TPU v7x, 32 devices: a whole 2x2x4 slice. The times are simulated.
32 devices in a mesh: groups: 2 (over y), shard: 4 (over z), dp: 4 (over x, core).
Axes of the slice: x: 2, y: 2, z: 4, core: 2. Of those that a mesh axis runs over, the one named last changes fastest.
Arguments:
- maps_in: bfloat16 [32, 32, 1536], P(('groups', 'dp')), parts along dimension 0, may hold values from -6 to 6
- filters: bfloat16 [49, 1536], replicated, may hold values from -2 to 2
- w_expand: bfloat16 [1536, 6144], P(None, 'shard'), may hold values from -0.15625 to 0.15625
- w_project: bfloat16 [6144, 1536], P('shard'), may hold values from -0.078125 to 0.078125
- cotangent: bfloat16 [32, 32, 1536], P(('groups', 'dp')), parts along dimension 0, may hold values from -6 to 6
Outputs:
- block_out: bfloat16 [32, 32, 1536], P(('groups', 'dp')), parts along dimension 0
- grad_input: bfloat16 [32, 32, 1536], P(('groups', 'dp')), parts along dimension 0
- grad_expand: float32 [3072, 6144], P(('groups', 'dp'), 'shard'), parts along dimension 0
- grad_project: float32 [12288, 1536], P(('groups', 'shard'), 'dp'), parts along dimension 0
- grad_filters: float32 [98, 1536], P('groups'), parts along dimension 0
There are 2 independent parts, one for each index of `groups`. A program takes and returns all parts, laid end to end along the dimension named above; an argument that names none is the same for every part. Nothing has to cross between parts.
All inputs are finite; a program needn't handle non-finite values.
Results may differ from a plain program's by a relative error of at most 0.015.
Values may be sent and summed in bfloat16 or wider, within the bound.
A program may use at most 128 MiB of HBM per device.

v0:
```python
import jax
import jax.numpy as jnp
from jax import lax
from jax.sharding import PartitionSpec as P

KS = 7


def extended(block, sides, width):
    for axis, dim in sides:
        count = lax.axis_size(axis)
        forward = [(i, i + 1) for i in range(count - 1)]
        backward = [(target, source) for source, target in forward]
        low = lax.ppermute(
            lax.slice_in_dim(block, block.shape[dim] - width, None, axis=dim), axis, forward
        )
        high = lax.ppermute(lax.slice_in_dim(block, 0, width, axis=dim), axis, backward)
        block = jnp.concatenate([low, block, high], axis=dim)
    return block


def gelu_parts(hidden):
    cdf = 0.5 * (1.0 + jax.scipy.special.erf(hidden * 0.7071067811865476))
    density = jnp.exp(-0.5 * hidden * hidden) * 0.3989422804014327
    return (hidden * cdf, cdf + hidden * density)


def norm_stats(conv_rows):
    centered = conv_rows - jnp.mean(conv_rows, axis=-1, keepdims=True)
    variance = jnp.mean(centered * centered, axis=-1, keepdims=True)
    inv_scale = lax.rsqrt(variance + 1e-06)
    return (centered * inv_scale, inv_scale)


def norm_back(d_normed, scaled, inv_scale):
    first = jnp.mean(d_normed, axis=-1, keepdims=True)
    second = jnp.mean(d_normed * scaled, axis=-1, keepdims=True)
    return inv_scale * (d_normed - first - scaled * second)


def body(maps_in, filters, w_expand, w_project, cotangent):
    reach = KS // 2
    rows, cols, width = maps_in.shape
    count = rows * cols
    taps_f32 = filters.astype(jnp.float32)
    halo_in = extended(maps_in, (("dp", 0),), reach)
    padded_in = jnp.pad(halo_in, ((0, 0), (reach, reach), (0, 0)))
    conv_out = jnp.zeros((rows, cols, width), jnp.float32)
    for tap in range(KS * KS):
        tap_row, tap_col = divmod(tap, KS)
        conv_out = (
            conv_out
            + padded_in[tap_row : tap_row + rows, tap_col : tap_col + cols].astype(jnp.float32)
            * taps_f32[tap]
        )
    scaled, inv_scale = norm_stats(conv_out.reshape(count, width))
    normed = scaled.astype(jnp.bfloat16)
    hidden = jnp.dot(normed, w_expand, preferred_element_type=jnp.float32)
    activ, slope = gelu_parts(hidden)
    act = activ.astype(jnp.bfloat16)
    partial_out = jnp.dot(act, w_project, preferred_element_type=jnp.float32)
    cot_rows = cotangent.reshape(count, width)
    summed_out = lax.psum(partial_out.astype(jnp.bfloat16), "shard").astype(jnp.float32)
    d_act = lax.dot_general(
        cot_rows, w_project, (((1,), (1,)), ((), ())), preferred_element_type=jnp.float32
    )
    d_hidden = (d_act * slope).astype(jnp.bfloat16)
    grad_proj_local = lax.dot_general(
        act, cot_rows, (((0,), (0,)), ((), ())), preferred_element_type=jnp.float32
    )
    grad_exp_local = lax.dot_general(
        normed, d_hidden, (((0,), (0,)), ((), ())), preferred_element_type=jnp.float32
    )
    partial_norm = lax.dot_general(
        d_hidden, w_expand, (((1,), (1,)), ((), ())), preferred_element_type=jnp.float32
    )
    d_normed = lax.psum(partial_norm.astype(jnp.bfloat16), "shard").astype(jnp.float32)
    d_conv = norm_back(d_normed, scaled, inv_scale).astype(jnp.bfloat16)
    block_out = (
        (maps_in.reshape(count, width).astype(jnp.float32) + summed_out)
        .astype(jnp.bfloat16)
        .reshape(rows, cols, width)
    )
    grad_expand, grad_project = (
        lax.psum_scatter(
            grad_exp_local.astype(jnp.bfloat16), "dp", scatter_dimension=0, tiled=True
        ).astype(jnp.float32),
        lax.psum_scatter(
            grad_proj_local.astype(jnp.bfloat16), "dp", scatter_dimension=1, tiled=True
        ).astype(jnp.float32),
    )
    d_conv = d_conv.reshape(rows, cols, width)
    halo_grad = extended(d_conv, (("dp", 0),), reach)
    padded_grad = jnp.pad(halo_grad, ((0, 0), (reach, reach), (0, 0)))
    conv_grad = d_conv.astype(jnp.float32)
    back_sum = cotangent.astype(jnp.float32)
    filter_rows = []
    for tap in range(KS * KS):
        tap_row, tap_col = divmod(tap, KS)
        back_sum = (
            back_sum
            + padded_grad[
                2 * reach - tap_row : 2 * reach - tap_row + rows,
                2 * reach - tap_col : 2 * reach - tap_col + cols,
            ].astype(jnp.float32)
            * taps_f32[tap]
        )
        filter_rows.append(
            jnp.sum(
                conv_grad
                * padded_in[tap_row : tap_row + rows, tap_col : tap_col + cols].astype(jnp.float32),
                axis=(0, 1),
            )
        )
    grad_input = back_sum.astype(jnp.bfloat16)
    grad_filters = lax.psum(jnp.stack(filter_rows, axis=0).astype(jnp.bfloat16), "dp").astype(
        jnp.float32
    )
    return (block_out, grad_input, grad_expand, grad_project, grad_filters)


def solution(mesh):
    placed = (
        P(("groups", "dp"), None, None),
        P(),
        P(None, "shard"),
        P("shard", None),
        P(("groups", "dp"), None, None),
    )
    return jax.shard_map(
        body,
        mesh=mesh,
        in_specs=placed,
        out_specs=(
            P(("groups", "dp"), None, None),
            P(("groups", "dp"), None, None),
            P(("groups", "dp"), "shard"),
            P(("groups", "shard"), "dp"),
            P("groups", None),
        ),
        check_vma=False,
    )
```

profile of v0, /device:TPU:0, one launch (start us, length us, event | category | flops | bytes accessed | tf_op | source)
XLA Modules:
  0.0 244.9 jit_solution(9113310455872859118)
XLA Ops:
  7.2 0.0 all-reduce.8.cloned.1.call-start
  7.2 1.1 fusion.145
  8.4 2.4 collective-permute-start
  10.7 1.3 collective-permute-start.1
  12.0 0.9 convert_element_type.408
  13.0 0.2 slice_reduce_fusion.46
  13.2 0.3 slice_reduce_fusion.48
  13.7 0.9 slice_reduce_fusion.47
  14.8 0.1 constant_dynamic-update-slice_fusion
  14.9 1.4 collective-permute-done.1
  16.3 0.4 select_maximum_fusion.2
  16.9 9.2 %fusion.142 = (f32[4,32]{1,0:T(4,128)S(1)}, f32[4,32,1536]{2,1,0:T(8,128)S(1)}) fusion(f32[1536]{0:T(1024)S(1)} %get-tuple-element.66, bf16[10,38,1536]{2,1,0:T(8,128)(2,1)S(1)} %select_maximum_fusion.2, f32[1536]{0:T(1024)S(1)} %get-tuple-element.67, f32[1536]{0:T(1024)S(1)} %get-tuple-element.68, f32[1536]{0:T(1024)S(1)} %get-tuple-element.69, ...), kind=kLoop, calls=%fused_computation.326 | loop fusion | flops 28901248 | bytes 20355584 | tf_op jit(solution)/shard_map/reduce_sum | solution.py:29
  26.3 0.6 div.15
  26.9 0.2 multiply_reduce_fusion
  27.1 0.6 rsqrt.12
  27.7 0.9 fusion.136
  28.7 3.6 %fusion.146 = f32[128,1536]{1,0:T(8,128)S(1)} fusion(bf16[128,1536]{1,0:T(8,128)(2,1)S(1)} %fusion.136, bf16[1536,1536]{1,0:T(8,128)(2,1)} %param.7), kind=kOutput, calls=%fused_computation.329 | convolution fusion | flops 603979776 | bytes 5898240 | tf_op jit(solution)/shard_map/dot_general | solution.py:58
  32.3 4.2 %convolution_convert_fusion.3 = bf16[128,1536]{1,0:T(8,128)(2,1)} fusion(bf16[1536,1536]{1,0:T(8,128)(2,1)} %param.8, f32[128,1536]{1,0:T(8,128)S(1)} %fusion.146), kind=kOutput, calls=%fused_computation.57 | convolution fusion | flops 605159424 | bytes 5898240 | tf_op jit(solution)/shard_map/dot_general | solution.py:61
  36.6 1.7 fusion.1
  38.3 2.4 convolution_convert_fusion.2
  40.7 0.0 all-reduce.8.cloned.1.call-update
  40.7 0.2 all-reduce.6.cloned.1.call-start
  40.9 49.0 %all-reduce.8.cloned.1.call-done = (bf16[128,1536]{1,0:T(8,128)(2,1)}, bf16[128,1536]{1,0:T(8,128)(2,1)}) async-done(((bf16[128,1536]{1,0:T(8,128)(2,1)}, bf16[128,1536]{1,0:T(8,128)(2,1)}), (bf16[128,1536]{1,0:T(8,128)(2,1)}, bf16[128,1536]{1,0:T(8,128)(2,1)})) %all-reduce.8.cloned.1.call-update) | async-done | bytes 786448 | tf_op jit(solution)/shard_map/psum | solution.py:63
  89.9 1.3 convert_reduce_fusion
  91.2 3.5 %fusion.132 = (bf16[1536]{0:T(1024)(128)(2,1)S(1)}, bf16[1536]{0:T(1024)(128)(2,1)S(1)}, bf16[1536]{0:T(1024)(128)(2,1)S(1)}, bf16[1536]{0:T(1024)(128)(2,1)S(1)...) fusion(bf16[10,38,1536]{2,1,0:T(8,128)(2,1)S(1)} %select_maximu, ...), kind=kLoop, calls=%fused_computation.249 | loop fusion | flops 12358656 | bytes 8708096 | tf_op jit(solution)/shard_map/reduce_sum | solution.py:109
  94.8 1.2 fusion.129
  96.0 2.0 fusion.111
  98.7 4.8 %stack.249 = bf16[49,1536]{1,0:T(8,128)(2,1)} concatenate(bf16[1,1536]{1,0:T(2,128)(2,1)S(1)} %stack.200, bf16[1,1536]{1,0:T(2,128)(2,1)S(1)} %stack.201, bf16[1,1536]{1,0:T(2,128)(2,1)S(1)} %stack.202, bf16[1,1536]{1,0:T(2,128)(2,1)S(1)} %stack.203, bf16[1,1536]{1,0:T(2,128)(2,1)S(1)} %stack.204, bf16[1,1536]{1,0:T(2,128)(2,1)S(1)} %stack.205, bf16[1,1536]{1,0:T(2,128)(2,1)S(1)} %stack.206, ...), dimensions={0} | concatenate | bytes 301056 | tf_op jit(solution)/shard_map/stack | solution.py:116
  103.5 0.0 reduce-scatter.7.cloned.1.call-start
  103.6 3.6 %convolution_convert_fusion = bf16[1536,1536]{1,0:T(8,128)(2,1)} fusion(bf16[128,1536]{1,0:T(8,128)(2,1)S(1)} %bitcast.89, f32[128,1536]{1,0:T(8,128)S(1)} %copy-done.2), kind=kOutput, calls=%fused_computation.50 | convolution fusion | flops 607322112 | bytes 5898240 | tf_op jit(solution)/shard_map/dot_general | solution.py:68
  107.2 6.6 %copy.10 = bf16[1536,1536]{0,1:T(8,128)(2,1)} copy(bf16[1536,1536]{1,0:T(8,128)(2,1)} %convolution_convert_fusion) | data formatting | bytes 9437184
  113.9 0.0 reduce-scatter.7.cloned.1.call-update
  113.9 0.0 reduce-scatter.5.cloned.1.call-start
  113.9 0.9 copy-done.6
  114.8 0.1 copy-done.10
  115.0 3.6 %convolution_convert_fusion.1 = bf16[1536,1536]{1,0:T(8,128)(2,1)} fusion(bf16[128,1536]{1,0:T(8,128)(2,1)S(1)} %copy-done.6, bf16[128,1536]{1,0:T(8,128)(2,1)S(1)} %copy-done.10), kind=kOutput, calls=%fused_computation.51 | convolution fusion | flops 606339072 | bytes 5505024 | tf_op jit(solution)/shard_map/dot_general | solution.py:71
  119.0 1.9 collective-permute-start.2
  120.9 1.3 collective-permute-start.3
  122.2 0.8 fusion.134
  123.1 10.1 %all-reduce.6.cloned.1.call-done = bf16[49,1536]{1,0:T(8,128)(2,1)} async-done(((bf16[49,1536]{1,0:T(8,128)(2,1)}), bf16[49,1536]{1,0:T(8,128)(2,1)}) %all-reduce.6.cloned.1.call-update) | async-done | bytes 150544 | tf_op jit(solution)/shard_map/psum | solution.py:116
  133.2 1.7 convert_element_type.521
  134.8 0.4 select_maximum_fusion
  135.6 7.4 %fusion.135 = bf16[4,32,1536]{2,1,0:T(8,128)(2,1)} fusion(bf16[4,32,1536]{2,1,0:T(8,128)(2,1)S(1)} %bitcast.85, bf16[4,32,1536]{2,1,0:T(8,128)(2,1)S(1)} %copy-done.8, bf16[3,32,1536]{2,1,0:T(8,128)(2,1)S(1)} %collective-permute-done.2, bf16[3,32,1536]{2,1,0:T(8,128)(2,1)S(1)} %collective-permute-done.3, bf16[10,38,1536]{2,1,0:T(8,128)(2,1)S(1)} %select_maximum_fusion, ...), kind=kLoop, calls=%fused_computation.257 | loop fusion | flops 30474240 | bytes 18585600 | tf_op jit(solution)/shard_map/convert_element_type | solution.py:115
  142.9 42.2 %reduce-scatter.7.cloned.1.call-done = bf16[384,1536]{1,0:T(8,128)(2,1)} async-done(((bf16[1536,1536]{1,0:T(8,128)(2,1)}), bf16[384,1536]{1,0:T(8,128)(2,1)}) %reduce-scatter.7.cloned.1.call-update) | async-done | bytes 1179664
  185.1 1.7 copy.11
  186.8 1.6 convert_element_type.520
  188.4 47.0 %reduce-scatter.5.cloned.1.call-done = bf16[384,1536]{1,0:T(8,128)(2,1)} async-done(((bf16[1536,1536]{1,0:T(8,128)(2,1)}), bf16[384,1536]{1,0:T(8,128)(2,1)}) %reduce-scatter.5.cloned.1.call-update) | async-done | bytes 1179664 | tf_op jit(solution)/shard_map/reduce_scatter | solution.py:85
  235.4 3.0 %convert_element_type.518 = f32[384,1536]{1,0:T(8,128)} convert(bf16[384,1536]{1,0:T(8,128)(2,1)} %reduce-scatter.5.cloned.1.call-done) | non-fusion elementwise | flops 589824 | bytes 3538944 | tf_op jit(solution)/shard_map/convert_element_type | solution.py:87
  (244 shorter events, 0.9 us)
Async XLA Ops:
  7.2 82.7 %all-reduce.8.cloned.1.call-start = ((), (), s32[]{:S(2)}) async-start(), calls=%async_computation.5 | async-start | bytes 1572864 | tf_op jit(solution)/shard_map/psum | solution.py:63
  8.4 6.4 %collective-permute-start = (bf16[3,32,1536]{2,1,0:T(8,128)(2,1)S(1)}, bf16[3,32,1536]{2,1,0:T(8,128)(2,1)S(1)}, u32[]{:S(2)}, u32[]{:S(2)}) collective-permute-start(bf16[3,32,1536]{2,1,0:T(8,128)(2,1)S(1)} %get-tuple-element.123), channel_id=1, source_target_pairs={{0,1},{1,2},{2,3},{4,5},{5,6},{6,7},{8,9},{9,10},{10,11},{12,13},{... | collective-permute-start | bytes 884744 | tf_op jit(solution)/shard_map/ppermute | solution.py:14
  10.7 5.6 %collective-permute-start.1 = (bf16[3,32,1536]{2,1,0:T(8,128)(2,1)S(1)}, bf16[3,32,1536]{2,1,0:T(8,128)(2,1)S(1)}, u32[]{:S(2)}, u32[]{:S(2)}) collective-permute-start(bf16[3,32,1536]{2,1,0:T(8,128)(2,1)S(1)} %get-tuple-element.124), channel_id=1, source_target_pairs={{1,0},{2,1},{3,2},{5,4},{6,5},{7,6},{9,8},{10,9},{11,10},{13,12},{... | collective-permute-start | bytes 884744 | tf_op jit(solution)/shard_map/ppermute | solution.py:17
  14.6 11.5 %copy-start.66 = (f32[1536]{0:T(1024)}, f32[1536]{0:T(1024)S(1)}, u32[]{:S(2)}) copy-start(f32[1536]{0:T(1024)S(1)} %get-tuple-element.89) | copy-start | bytes 18436
  14.6 11.5 %copy-start.68 = (f32[1536]{0:T(1024)}, f32[1536]{0:T(1024)S(1)}, u32[]{:S(2)}) copy-start(f32[1536]{0:T(1024)S(1)} %get-tuple-element.90) | copy-start | bytes 18436
  40.7 92.5 %all-reduce.6.cloned.1.call-start = ((), (), s32[]{:S(2)}) async-start(), calls=%async_computation.3 | async-start | bytes 344064 | tf_op jit(solution)/shard_map/psum | solution.py:116
  103.5 81.6 %reduce-scatter.7.cloned.1.call-start = ((), (), s32[]{:S(2)}) async-start(), calls=%async_computation.4 | async-start | bytes 5898240
  113.9 121.5 %reduce-scatter.5.cloned.1.call-start = ((), (), s32[]{:S(2)}) async-start(), calls=%async_computation.2 | async-start | bytes 5898240 | tf_op jit(solution)/shard_map/reduce_scatter | solution.py:85
  118.6 16.6 %copy-start.13 = (f32[1536]{0:T(1024)S(1)}, f32[1536]{0:T(1024)}, u32[]{:S(2)}) copy-start(f32[1536]{0:T(1024)} %copy-done.12) | copy-start | bytes 18436
  118.6 16.6 %copy-start.15 = (f32[1536]{0:T(1024)S(1)}, f32[1536]{0:T(1024)}, u32[]{:S(2)}) copy-start(f32[1536]{0:T(1024)} %copy-done.14) | copy-start | bytes 18436
  118.6 16.6 %copy-start.17 = (f32[1536]{0:T(1024)S(1)}, f32[1536]{0:T(1024)}, u32[]{:S(2)}) copy-start(f32[1536]{0:T(1024)} %copy-done.16) | copy-start | bytes 18436
  118.6 16.6 %copy-start.19 = (f32[1536]{0:T(1024)S(1)}, f32[1536]{0:T(1024)}, u32[]{:S(2)}) copy-start(f32[1536]{0:T(1024)} %copy-done.18) | copy-start | bytes 18436
  118.6 16.6 %copy-start.21 = (f32[1536]{0:T(1024)S(1)}, f32[1536]{0:T(1024)}, u32[]{:S(2)}) copy-start(f32[1536]{0:T(1024)} %copy-done.20) | copy-start | bytes 18436
  118.6 16.6 %copy-start.23 = (f32[1536]{0:T(1024)S(1)}, f32[1536]{0:T(1024)}, u32[]{:S(2)}) copy-start(f32[1536]{0:T(1024)} %copy-done.22) | copy-start | bytes 18436
  118.6 16.6 %copy-start.25 = (f32[1536]{0:T(1024)S(1)}, f32[1536]{0:T(1024)}, u32[]{:S(2)}) copy-start(f32[1536]{0:T(1024)} %copy-done.24) | copy-start | bytes 18436
  118.6 16.6 %copy-start.27 = (f32[1536]{0:T(1024)S(1)}, f32[1536]{0:T(1024)}, u32[]{:S(2)}) copy-start(f32[1536]{0:T(1024)} %copy-done.26) | copy-start | bytes 18436
  118.7 16.6 %copy-start.29 = (f32[1536]{0:T(1024)S(1)}, f32[1536]{0:T(1024)}, u32[]{:S(2)}) copy-start(f32[1536]{0:T(1024)} %copy-done.28) | copy-start | bytes 18436
  118.7 16.6 %copy-start.31 = (f32[1536]{0:T(1024)S(1)}, f32[1536]{0:T(1024)}, u32[]{:S(2)}) copy-start(f32[1536]{0:T(1024)} %copy-done.30) | copy-start | bytes 18436
  118.7 16.6 %copy-start.33 = (f32[1536]{0:T(1024)S(1)}, f32[1536]{0:T(1024)}, u32[]{:S(2)}) copy-start(f32[1536]{0:T(1024)} %copy-done.32) | copy-start | bytes 18436
  118.7 16.6 %copy-start.35 = (f32[1536]{0:T(1024)S(1)}, f32[1536]{0:T(1024)}, u32[]{:S(2)}) copy-start(f32[1536]{0:T(1024)} %copy-done.34) | copy-start | bytes 18436
  118.7 16.6 %copy-start.37 = (f32[1536]{0:T(1024)S(1)}, f32[1536]{0:T(1024)}, u32[]{:S(2)}) copy-start(f32[1536]{0:T(1024)} %copy-done.36) | copy-start | bytes 18436
  118.7 16.6 %copy-start.39 = (f32[1536]{0:T(1024)S(1)}, f32[1536]{0:T(1024)}, u32[]{:S(2)}) copy-start(f32[1536]{0:T(1024)} %copy-done.38) | copy-start | bytes 18436
  118.7 16.6 %copy-start.41 = (f32[1536]{0:T(1024)S(1)}, f32[1536]{0:T(1024)}, u32[]{:S(2)}) copy-start(f32[1536]{0:T(1024)} %copy-done.40) | copy-start | bytes 18436
  118.7 16.6 %copy-start.43 = (f32[1536]{0:T(1024)S(1)}, f32[1536]{0:T(1024)}, u32[]{:S(2)}) copy-start(f32[1536]{0:T(1024)} %copy-done.42) | copy-start | bytes 18436
  118.7 16.6 %copy-start.45 = (f32[1536]{0:T(1024)S(1)}, f32[1536]{0:T(1024)}, u32[]{:S(2)}) copy-start(f32[1536]{0:T(1024)} %copy-done.44) | copy-start | bytes 18436
  118.7 16.6 %copy-start.47 = (f32[1536]{0:T(1024)S(1)}, f32[1536]{0:T(1024)}, u32[]{:S(2)}) copy-start(f32[1536]{0:T(1024)} %copy-done.46) | copy-start | bytes 18436
  118.8 16.6 %copy-start.49 = (f32[1536]{0:T(1024)S(1)}, f32[1536]{0:T(1024)}, u32[]{:S(2)}) copy-start(f32[1536]{0:T(1024)} %copy-done.48) | copy-start | bytes 18436
  118.8 16.6 %copy-start.51 = (f32[1536]{0:T(1024)S(1)}, f32[1536]{0:T(1024)}, u32[]{:S(2)}) copy-start(f32[1536]{0:T(1024)} %copy-done.50) | copy-start | bytes 18436
  118.8 16.6 %copy-start.53 = (f32[1536]{0:T(1024)S(1)}, f32[1536]{0:T(1024)}, u32[]{:S(2)}) copy-start(f32[1536]{0:T(1024)} %copy-done.52) | copy-start | bytes 18436
  118.8 16.6 %copy-start.55 = (f32[1536]{0:T(1024)S(1)}, f32[1536]{0:T(1024)}, u32[]{:S(2)}) copy-start(f32[1536]{0:T(1024)} %copy-done.54) | copy-start | bytes 18436
  118.8 16.6 %copy-start.57 = (f32[1536]{0:T(1024)S(1)}, f32[1536]{0:T(1024)}, u32[]{:S(2)}) copy-start(f32[1536]{0:T(1024)} %copy-done.56) | copy-start | bytes 18436
  118.8 16.6 %copy-start.59 = (f32[1536]{0:T(1024)S(1)}, f32[1536]{0:T(1024)}, u32[]{:S(2)}) copy-start(f32[1536]{0:T(1024)} %copy-done.58) | copy-start | bytes 18436
  118.8 16.6 %copy-start.61 = (f32[1536]{0:T(1024)S(1)}, f32[1536]{0:T(1024)}, u32[]{:S(2)}) copy-start(f32[1536]{0:T(1024)} %copy-done.60) | copy-start | bytes 18436
  118.8 16.6 %copy-start.63 = (f32[1536]{0:T(1024)S(1)}, f32[1536]{0:T(1024)}, u32[]{:S(2)}) copy-start(f32[1536]{0:T(1024)} %copy-done.62) | copy-start | bytes 18436
  118.8 16.6 %copy-start.65 = (f32[1536]{0:T(1024)S(1)}, f32[1536]{0:T(1024)}, u32[]{:S(2)}) copy-start(f32[1536]{0:T(1024)} %copy-done.64) | copy-start | bytes 18436
  118.8 16.6 %copy-start.67 = (f32[1536]{0:T(1024)S(1)}, f32[1536]{0:T(1024)}, u32[]{:S(2)}) copy-start(f32[1536]{0:T(1024)} %copy-done.66) | copy-start | bytes 18436
  118.9 16.6 %copy-start.69 = (f32[1536]{0:T(1024)S(1)}, f32[1536]{0:T(1024)}, u32[]{:S(2)}) copy-start(f32[1536]{0:T(1024)} %copy-done.68) | copy-start | bytes 18436
  118.9 16.6 %copy-start.71 = (f32[1536]{0:T(1024)S(1)}, f32[1536]{0:T(1024)}, u32[]{:S(2)}) copy-start(f32[1536]{0:T(1024)} %copy-done.70) | copy-start | bytes 18436
  118.9 16.6 %copy-start.73 = (f32[1536]{0:T(1024)S(1)}, f32[1536]{0:T(1024)}, u32[]{:S(2)}) copy-start(f32[1536]{0:T(1024)} %copy-done.72) | copy-start | bytes 18436
  118.9 16.6 %copy-start.75 = (f32[1536]{0:T(1024)S(1)}, f32[1536]{0:T(1024)}, u32[]{:S(2)}) copy-start(f32[1536]{0:T(1024)} %copy-done.74) | copy-start | bytes 18436
  118.9 16.6 %copy-start.77 = (f32[1536]{0:T(1024)S(1)}, f32[1536]{0:T(1024)}, u32[]{:S(2)}) copy-start(f32[1536]{0:T(1024)} %copy-done.76) | copy-start | bytes 18436
  118.9 16.6 %copy-start.79 = (f32[1536]{0:T(1024)S(1)}, f32[1536]{0:T(1024)}, u32[]{:S(2)}) copy-start(f32[1536]{0:T(1024)} %copy-done.78) | copy-start | bytes 18436
  118.9 16.6 %copy-start.81 = (f32[1536]{0:T(1024)S(1)}, f32[1536]{0:T(1024)}, u32[]{:S(2)}) copy-start(f32[1536]{0:T(1024)} %copy-done.80) | copy-start | bytes 18436
  118.9 16.6 %copy-start.83 = (f32[1536]{0:T(1024)S(1)}, f32[1536]{0:T(1024)}, u32[]{:S(2)}) copy-start(f32[1536]{0:T(1024)} %copy-done.82) | copy-start | bytes 18436
  118.9 16.6 %copy-start.85 = (f32[1536]{0:T(1024)S(1)}, f32[1536]{0:T(1024)}, u32[]{:S(2)}) copy-start(f32[1536]{0:T(1024)} %copy-done.84) | copy-start | bytes 18436
  118.9 16.6 %copy-start.87 = (f32[1536]{0:T(1024)S(1)}, f32[1536]{0:T(1024)}, u32[]{:S(2)}) copy-start(f32[1536]{0:T(1024)} %copy-done.86) | copy-start | bytes 18436
  119.0 15.8 %collective-permute-start.2 = (bf16[3,32,1536]{2,1,0:T(8,128)(2,1)S(1)}, bf16[3,32,1536]{2,1,0:T(8,128)(2,1)S(1)}, u32[]{:S(2)}, u32[]{:S(2)}) collective-permute-start(bf16[3,32,1536]{2,1,0:T(8,128)(2,1)S(1)} %bitcast.93), channel_id=1, source_target_pairs={{0,1},{1,2},{2,3},{4,5},{5,6},{6,7},{8,9},{9,10},{10,11},{12,13},{... | collective-permute-start | bytes 884744 | tf_op jit(solution)/shard_map/ppermute | solution.py:14
  120.9 13.9 %collective-permute-start.3 = (bf16[3,32,1536]{2,1,0:T(8,128)(2,1)S(1)}, bf16[3,32,1536]{2,1,0:T(8,128)(2,1)S(1)}, u32[]{:S(2)}, u32[]{:S(2)}) collective-permute-start(bf16[3,32,1536]{2,1,0:T(8,128)(2,1)S(1)} %bitcast.92), channel_id=1, source_target_pairs={{1,0},{2,1},{3,2},{5,4},{6,5},{7,6},{9,8},{10,9},{11,10},{13,12},{... | collective-permute-start | bytes 884744 | tf_op jit(solution)/shard_map/ppermute | solution.py:17
  (52 other events, 323.0 us)
Sparse Core Ops, SparseCore 0:
  40.8 49.0 all-reduce.7
  103.6 29.4 all-reduce.5
  135.9 49.2 reduce-scatter.6
  187.5 47.8 reduce-scatter.4
where the time goes:
time: 245 us
  waiting for transfers between devices  150 us (61%)
  other arithmetic  34.5 us (14%)
  matrix products  19 us (8%)
  local copies, waits for them, and re-layouts  18.7 us (8%)
  between operations  15.7 us (6%)
  starting transfers between devices  7.21 us (3%)
    psum x1, waiting for transfers between devices, body(): lax.psum(partial_out.astype(jnp.bfloat16), 'shard').astype(jnp.float32)  49 us
    reduce_scatter x1, waiting for transfers between devices, body(): lax.psum_scatter(grad_exp_local.astype(jnp.bfloat16), 'dp', scatter_dimen...  47 us
    unnamed x5, waiting for transfers between devices  42.3 us
    psum x1, waiting for transfers between devices, body(): lax.psum(jnp.stack(filter_rows, axis=0).astype(jnp.bfloat16), 'dp')  10.1 us
    unnamed x187, local copies, waits for them, and re-layouts  9.8 us
    reduce_sum x1, other arithmetic, norm_stats(): centered = conv_rows - jnp.mean(conv_rows, axis=-1, keepdims=True)  9.17 us
    convert_element_type x1, other arithmetic, body(): grad_input = back_sum.astype(jnp.bfloat16)  7.36 us
    reduce_sum x3, other arithmetic, body(): jnp.sum(conv_grad * padded_in[tap_row:tap_row + rows, tap_col:tap_col + c...  6.76 us
  transfers between devices with their start and end apart: 8, of which 5 were waited for; matrix products, arithmetic and copies ran while one was open for 12% of the time, Pallas kernels for 0%

commit v1 on v0

--- a/solution.py
+++ b/solution.py
@@ -113,9 +113,9 @@
             )
         )
     grad_input = back_sum.astype(jnp.bfloat16)
-    grad_filters = lax.psum(jnp.stack(filter_rows, axis=0).astype(jnp.bfloat16), "dp").astype(
-        jnp.float32
-    )
+    grad_filters = jnp.sum(
+        lax.all_gather(jnp.stack(filter_rows, axis=0).astype(jnp.bfloat16), "dp"), axis=0
+    ).astype(jnp.float32)
     return (block_out, grad_input, grad_expand, grad_project, grad_filters)
 
 

time: 245 us -> 171 us (0.70)
  waiting for transfers between devices: 150 us -> 67.2 us
  blocking collectives: 0 us -> 9.04 us
  local copies, waits for them, and re-layouts: 18.7 us -> 14.2 us
    unnamed x5 -> x4, waiting for transfers between devices: 42.3 us -> 0.05 us
    psum x1, waiting for transfers between devices: 49 us -> 32.8 us  [body(): lax.psum(partial_out.astype(jnp.bfloat16), 'shard').astype(jnp.float32)]
    reduce_scatter x1, waiting for transfers between devices: 47 us -> 31.5 us  [body(): lax.psum_scatter(grad_exp_local.astype(jnp.bfloat16), 'dp', scatter_dimen...]
    psum x1 -> x0, waiting for transfers between devices: 10.1 us -> none  [body(): lax.psum(jnp.stack(filter_rows, axis=0).astype(jnp.bfloat16), 'dp')]
    all_gather x0 -> x1, blocking collectives: none -> 9.04 us  [body(): lax.all_gather(jnp.stack(filter_rows, axis=0).astype(jnp.bfloat16), 'dp')]
    another operation x50, local copies, waits for them, and re-layouts: 5.07 us -> 0.86 us  [body(): jnp.stack(filter_rows, axis=0).astype(jnp.bfloat16)]
    unnamed x187 -> x183, local copies, waits for them, and re-layouts: 9.8 us -> 9.49 us
  transfers between devices with their start and end apart: 8 -> 7, of which waited for: 5 -> 4; matrix products, arithmetic and copies ran while one was open for 12% -> 24% of each run, Pallas kernels for 0% -> 0%
where the time goes in v1:
time: 171 us; the launch traced here: 170 us
  waiting for transfers between devices  67.2 us (39%)
  other arithmetic  33.7 us (20%)
  matrix products  21.1 us (12%)
  between operations  17.3 us (10%)
  local copies, waits for them, and re-layouts  14.2 us (8%)
  blocking collectives  9.04 us (5%)
  starting transfers between devices  7.54 us (4%)
    psum x1, waiting for transfers between devices, body(): lax.psum(partial_out.astype(jnp.bfloat16), 'shard').astype(jnp.float32)  32.8 us
    reduce_scatter x1, waiting for transfers between devices, body(): lax.psum_scatter(grad_exp_local.astype(jnp.bfloat16), 'dp', scatter_dimen...  31.5 us
    unnamed x183, local copies, waits for them, and re-layouts  9.49 us
    reduce_sum x1, other arithmetic, norm_stats(): centered = conv_rows - jnp.mean(conv_rows, axis=-1, keepdims=True)  9.17 us
    all_gather x1, blocking collectives, body(): lax.all_gather(jnp.stack(filter_rows, axis=0).astype(jnp.bfloat16), 'dp')  9.04 us
    convert_element_type x1, other arithmetic, body(): grad_input = back_sum.astype(jnp.bfloat16)  7.37 us
    reduce_sum x3, other arithmetic, body(): jnp.sum(conv_grad * padded_in[tap_row:tap_row + rows, tap_col:tap_col + c...  6.76 us
    dot_general x1, matrix products, body(): lax.dot_general(act, cot_rows, (((0,), (0,)), ((), ())), preferred_elemen...  4.84 us
  transfers between devices with their start and end apart: 7, of which 4 were waited for; matrix products, arithmetic and copies ran while one was open for 24% of the time, Pallas kernels for 0%

profile of v1, /device:TPU:0, one launch (start us, length us, event | category | flops | bytes accessed | tf_op | source)
XLA Modules:
  0.0 170.1 jit_solution(13511883203734515055)
XLA Ops:
  8.0 0.0 all-reduce.5.cloned.1.call-start
  8.1 1.1 fusion.145
  9.2 2.4 %collective-permute-start = (bf16[3,32,1536]{2,1,0:T(8,128)(2,1)S(1)}, bf16[3,32,1536]{2,1,0:T(8,128)(2,1)S(1)}, u32[]{:S(2)}, u32[]{:S(2)}) collective-permute-start(bf16[3,32,1536]{2,1,0:T(8,128)(2,1)S(1)} %get-tuple-element.123), channel_id=1, source_target_pairs={{0,1},{1,2},{2,3},{4,5},{5,6},{6,7},{8,9},{9,10},{10,11},{12,13},{... | collective-permute-start | bytes 884744 | tf_op jit(solution)/shard_map/ppermute | solution.py:14
  11.6 1.3 collective-permute-start.1
  12.9 0.9 convert_element_type.417
  13.8 0.2 slice_reduce_fusion.46
  14.0 0.3 slice_reduce_fusion.48
  14.5 0.9 slice_reduce_fusion.47
  15.6 0.1 constant_dynamic-update-slice_fusion
  15.7 1.4 collective-permute-done.1
  17.1 0.4 select_maximum_fusion.2
  17.7 9.2 %fusion.142 = (f32[4,32]{1,0:T(4,128)S(1)}, f32[4,32,1536]{2,1,0:T(8,128)S(1)}) fusion(f32[1536]{0:T(1024)S(1)} %get-tuple-element.66, bf16[10,38,1536]{2,1,0:T(8,128)(2,1)S(1)} %select_maximum_fusion.2, f32[1536]{0:T(1024)S(1)} %get-tuple-element.67, f32[1536]{0:T(1024)S(1)} %get-tuple-element.68, f32[1536]{0:T(1024)S(1)} %get-tuple-element.69, ...), kind=kLoop, calls=%fused_computation.326 | loop fusion | flops 28901248 | bytes 20355584 | tf_op jit(solution)/shard_map/reduce_sum | solution.py:29
  27.1 0.6 div.15
  27.7 0.2 multiply_reduce_fusion
  27.9 0.6 rsqrt.12
  28.6 0.9 fusion.136
  29.5 3.5 %fusion.146 = f32[128,1536]{1,0:T(8,128)S(1)} fusion(bf16[128,1536]{1,0:T(8,128)(2,1)S(1)} %fusion.136, bf16[1536,1536]{1,0:T(8,128)(2,1)} %param.7), kind=kOutput, calls=%fused_computation.329 | convolution fusion | flops 603979776 | bytes 5898240 | tf_op jit(solution)/shard_map/dot_general | solution.py:58
  33.0 4.2 %convolution_convert_fusion.3 = bf16[128,1536]{1,0:T(8,128)(2,1)} fusion(bf16[1536,1536]{1,0:T(8,128)(2,1)} %param.8, f32[128,1536]{1,0:T(8,128)S(1)} %fusion.146), kind=kOutput, calls=%fused_computation.57 | convolution fusion | flops 605159424 | bytes 5898240 | tf_op jit(solution)/shard_map/dot_general | solution.py:61
  37.3 1.6 fusion.1
  38.9 0.8 copy-done.6
  39.7 2.4 %convolution_convert_fusion.2 = bf16[128,1536]{1,0:T(8,128)(2,1)} fusion(bf16[128,1536]{1,0:T(8,128)(2,1)S(1)} %fusion.1, bf16[1536,1536]{1,0:T(8,128)(2,1)S(1)} %bitcast.82), kind=kOutput, calls=%fused_computation.56 | convolution fusion | flops 604176384 | bytes 5505024 | tf_op jit(solution)/shard_map/dot_general | solution.py:74
  42.1 0.0 all-reduce.5.cloned.1.call-update
  42.1 0.0 reduce-scatter.7.cloned.1.call-start
  42.2 4.8 %convolution_convert_fusion = bf16[1536,1536]{1,0:T(8,128)(2,1)} fusion(bf16[128,1536]{1,0:T(8,128)(2,1)} %bitcast.88, f32[128,1536]{1,0:T(8,128)} %copy-done.1), kind=kOutput, calls=%fused_computation.50 | convolution fusion | flops 607322112 | bytes 5898240 | tf_op jit(solution)/shard_map/dot_general | solution.py:68
  47.0 6.6 %copy.10 = bf16[1536,1536]{0,1:T(8,128)(2,1)} copy(bf16[1536,1536]{1,0:T(8,128)(2,1)} %convolution_convert_fusion) | data formatting | bytes 9437184
  53.6 0.0 reduce-scatter.7.cloned.1.call-update
  53.6 0.2 reduce-scatter.5.cloned.1.call-start
  53.9 4.6 %convolution_convert_fusion.1 = bf16[1536,1536]{1,0:T(8,128)(2,1)} fusion(bf16[128,1536]{1,0:T(8,128)(2,1)S(1)} %fusion.136, bf16[128,1536]{1,0:T(8,128)(2,1)} %copy-done.6), kind=kOutput, calls=%fused_computation.51 | convolution fusion | flops 606339072 | bytes 5505024 | tf_op jit(solution)/shard_map/dot_general | solution.py:71
  58.5 0.0 reduce-scatter.5.cloned.1.call-update
  58.5 32.8 %all-reduce.5.cloned.1.call-done = (bf16[128,1536]{1,0:T(8,128)(2,1)}, bf16[128,1536]{1,0:T(8,128)(2,1)}) async-done(((bf16[128,1536]{1,0:T(8,128)(2,1)}, bf16[128,1536]{1,0:T(8,128)(2,1)}), (bf16[128,1536]{1,0:T(8,128)(2,1)}, bf16[128,1536]{1,0:T(8,128)(2,1)})) %all-reduce.5.cloned.1.call-update) | async-done | bytes 786448 | tf_op jit(solution)/shard_map/psum | solution.py:63
  91.3 1.3 convert_reduce_fusion
  92.6 3.5 %fusion.132 = (bf16[1536]{0:T(1024)(128)(2,1)S(1)}, bf16[1536]{0:T(1024)(128)(2,1)S(1)}, bf16[1536]{0:T(1024)(128)(2,1)S(1)}, bf16[1536]{0:T(1024)(128)(2,1)S(1)...) fusion(bf16[10,38,1536]{2,1,0:T(8,128)(2,1)S(1)} %select_maximu, ...), kind=kLoop, calls=%fused_computation.249 | loop fusion | flops 12358656 | bytes 8708096 | tf_op jit(solution)/shard_map/reduce_sum | solution.py:109
  96.2 1.2 fusion.129
  97.4 2.0 %fusion.111 = (bf16[1536]{0:T(1024)(128)(2,1)S(1)}, bf16[1536]{0:T(1024)(128)(2,1)S(1)}, bf16[1536]{0:T(1024)(128)(2,1)S(1)}, bf16[1536]{0:T(1024)(128)(2,1)S(1)...) fusion(bf16[10,38,1536]{2,1,0:T(8,128)(2,1)S(1)} %select_maximu, ...), kind=kLoop, calls=%fused_computation.228 | loop fusion | flops 10785792 | bytes 7526400 | tf_op jit(solution)/shard_map/reduce_sum | solution.py:109
  100.1 0.6 stack.199
  100.7 9.0 %all_gather.4 = bf16[4,49,1536]{2,1,0:T(8,128)(2,1)S(1)} all-gather(bf16[1,49,1536]{2,1,0:T(8,128)(2,1)S(1)} %stack.199), channel_id=1, replica_groups=mesh['groups'=2,'shard'=4,'dp'=4] {'dp'}, dimensions={0}, use_global_device_ids=true | all-gather | bytes 752640 | tf_op jit(solution)/shard_map/all_gather | solution.py:117
  109.7 0.1 reduce_sum.542
  110.2 0.8 convert_element_type.530
  111.0 2.3 %collective-permute-start.2 = (bf16[3,32,1536]{2,1,0:T(8,128)(2,1)S(1)}, bf16[3,32,1536]{2,1,0:T(8,128)(2,1)S(1)}, u32[]{:S(2)}, u32[]{:S(2)}) collective-permute-start(bf16[3,32,1536]{2,1,0:T(8,128)(2,1)S(1)} %bitcast.93), channel_id=1, source_target_pairs={{0,1},{1,2},{2,3},{4,5},{5,6},{6,7},{8,9},{9,10},{10,11},{12,13},{... | collective-permute-start | bytes 884744 | tf_op jit(solution)/shard_map/ppermute | solution.py:14
  113.3 1.3 collective-permute-start.3
  114.6 0.9 fusion.134
  115.5 1.3 collective-permute-done.3
  116.8 0.4 select_maximum_fusion
  117.6 7.4 %fusion.135 = bf16[4,32,1536]{2,1,0:T(8,128)(2,1)} fusion(bf16[4,32,1536]{2,1,0:T(8,128)(2,1)S(1)} %bitcast.85, bf16[4,32,1536]{2,1,0:T(8,128)(2,1)S(1)} %copy-done.5, bf16[3,32,1536]{2,1,0:T(8,128)(2,1)S(1)} %collective-permute-done.2, bf16[3,32,1536]{2,1,0:T(8,128)(2,1)S(1)} %collective-permute-done.3, bf16[10,38,1536]{2,1,0:T(8,128)(2,1)S(1)} %select_maximum_fusion, ...), kind=kLoop, calls=%fused_computation.257 | loop fusion | flops 30474240 | bytes 18585600 | tf_op jit(solution)/shard_map/convert_element_type | solution.py:115
  124.9 1.7 copy.11
  126.6 1.6 convert_element_type.529
  128.2 31.5 %reduce-scatter.5.cloned.1.call-done = bf16[384,1536]{1,0:T(8,128)(2,1)} async-done(((bf16[1536,1536]{1,0:T(8,128)(2,1)}), bf16[384,1536]{1,0:T(8,128)(2,1)}) %reduce-scatter.5.cloned.1.call-update) | async-done | bytes 1179664 | tf_op jit(solution)/shard_map/reduce_scatter | solution.py:85
  159.7 3.0 %convert_element_type.527 = f32[384,1536]{1,0:T(8,128)} convert(bf16[384,1536]{1,0:T(8,128)(2,1)} %reduce-scatter.5.cloned.1.call-done) | non-fusion elementwise | flops 589824 | bytes 3538944 | tf_op jit(solution)/shard_map/convert_element_type | solution.py:87
  (239 shorter events, 0.8 us)
Async XLA Ops:
  8.0 7.6 %copy-start = (bf16[4,32,1536]{2,1,0:T(8,128)(2,1)S(1)}, bf16[4,32,1536]{2,1,0:T(8,128)(2,1)}, u32[]{:S(2)}) copy-start(bf16[4,32,1536]{2,1,0:T(8,128)(2,1)} %param.5) | copy-start | bytes 1179652
  8.0 83.3 %all-reduce.5.cloned.1.call-start = ((), (), s32[]{:S(2)}) async-start(), calls=%async_computation.4 | async-start | bytes 1572864 | tf_op jit(solution)/shard_map/psum | solution.py:63
  9.2 6.4 %collective-permute-start = (bf16[3,32,1536]{2,1,0:T(8,128)(2,1)S(1)}, bf16[3,32,1536]{2,1,0:T(8,128)(2,1)S(1)}, u32[]{:S(2)}, u32[]{:S(2)}) collective-permute-start(bf16[3,32,1536]{2,1,0:T(8,128)(2,1)S(1)} %get-tuple-element.123), channel_id=1, source_target_pairs={{0,1},{1,2},{2,3},{4,5},{5,6},{6,7},{8,9},{9,10},{10,11},{12,13},{... | collective-permute-start | bytes 884744 | tf_op jit(solution)/shard_map/ppermute | solution.py:14
  11.6 5.6 %collective-permute-start.1 = (bf16[3,32,1536]{2,1,0:T(8,128)(2,1)S(1)}, bf16[3,32,1536]{2,1,0:T(8,128)(2,1)S(1)}, u32[]{:S(2)}, u32[]{:S(2)}) collective-permute-start(bf16[3,32,1536]{2,1,0:T(8,128)(2,1)S(1)} %get-tuple-element.124), channel_id=1, source_target_pairs={{1,0},{2,1},{3,2},{5,4},{6,5},{7,6},{9,8},{10,9},{11,10},{13,12},{... | collective-permute-start | bytes 884744 | tf_op jit(solution)/shard_map/ppermute | solution.py:17
  15.5 11.5 %copy-start.52 = (f32[1536]{0:T(1024)}, f32[1536]{0:T(1024)S(1)}, u32[]{:S(2)}) copy-start(f32[1536]{0:T(1024)S(1)} %get-tuple-element.84) | copy-start | bytes 18436
  15.5 11.5 %copy-start.54 = (f32[1536]{0:T(1024)}, f32[1536]{0:T(1024)S(1)}, u32[]{:S(2)}) copy-start(f32[1536]{0:T(1024)S(1)} %get-tuple-element.85) | copy-start | bytes 18436
  15.5 11.5 %copy-start.56 = (f32[1536]{0:T(1024)}, f32[1536]{0:T(1024)S(1)}, u32[]{:S(2)}) copy-start(f32[1536]{0:T(1024)S(1)} %get-tuple-element.86) | copy-start | bytes 18436
  15.5 11.5 %copy-start.58 = (f32[1536]{0:T(1024)}, f32[1536]{0:T(1024)S(1)}, u32[]{:S(2)}) copy-start(f32[1536]{0:T(1024)S(1)} %get-tuple-element.87) | copy-start | bytes 18436
  15.5 11.5 %copy-start.60 = (f32[1536]{0:T(1024)}, f32[1536]{0:T(1024)S(1)}, u32[]{:S(2)}) copy-start(f32[1536]{0:T(1024)S(1)} %get-tuple-element.88) | copy-start | bytes 18436
  15.5 11.5 %copy-start.62 = (f32[1536]{0:T(1024)}, f32[1536]{0:T(1024)S(1)}, u32[]{:S(2)}) copy-start(f32[1536]{0:T(1024)S(1)} %get-tuple-element.89) | copy-start | bytes 18436
  15.5 11.5 %copy-start.64 = (f32[1536]{0:T(1024)}, f32[1536]{0:T(1024)S(1)}, u32[]{:S(2)}) copy-start(f32[1536]{0:T(1024)S(1)} %get-tuple-element.90) | copy-start | bytes 18436
  15.5 11.5 %copy-start.66 = (f32[1536]{0:T(1024)}, f32[1536]{0:T(1024)S(1)}, u32[]{:S(2)}) copy-start(f32[1536]{0:T(1024)S(1)} %get-tuple-element.91) | copy-start | bytes 18436
  15.5 11.5 %copy-start.68 = (f32[1536]{0:T(1024)}, f32[1536]{0:T(1024)S(1)}, u32[]{:S(2)}) copy-start(f32[1536]{0:T(1024)S(1)} %get-tuple-element.92) | copy-start | bytes 18436
  15.5 11.5 %copy-start.70 = (f32[1536]{0:T(1024)}, f32[1536]{0:T(1024)S(1)}, u32[]{:S(2)}) copy-start(f32[1536]{0:T(1024)S(1)} %get-tuple-element.93) | copy-start | bytes 18436
  15.5 11.5 %copy-start.72 = (f32[1536]{0:T(1024)}, f32[1536]{0:T(1024)S(1)}, u32[]{:S(2)}) copy-start(f32[1536]{0:T(1024)S(1)} %get-tuple-element.94) | copy-start | bytes 18436
  15.5 11.5 %copy-start.74 = (f32[1536]{0:T(1024)}, f32[1536]{0:T(1024)S(1)}, u32[]{:S(2)}) copy-start(f32[1536]{0:T(1024)S(1)} %get-tuple-element.95) | copy-start | bytes 18436
  15.5 11.5 %copy-start.76 = (f32[1536]{0:T(1024)}, f32[1536]{0:T(1024)S(1)}, u32[]{:S(2)}) copy-start(f32[1536]{0:T(1024)S(1)} %get-tuple-element.96) | copy-start | bytes 18436
  15.5 11.5 %copy-start.78 = (f32[1536]{0:T(1024)}, f32[1536]{0:T(1024)S(1)}, u32[]{:S(2)}) copy-start(f32[1536]{0:T(1024)S(1)} %get-tuple-element.97) | copy-start | bytes 18436
  15.6 11.5 %copy-start.80 = (f32[1536]{0:T(1024)}, f32[1536]{0:T(1024)S(1)}, u32[]{:S(2)}) copy-start(f32[1536]{0:T(1024)S(1)} %get-tuple-element.98) | copy-start | bytes 18436
  15.6 11.5 %copy-start.82 = (f32[1536]{0:T(1024)}, f32[1536]{0:T(1024)S(1)}, u32[]{:S(2)}) copy-start(f32[1536]{0:T(1024)S(1)} %get-tuple-element.99) | copy-start | bytes 18436
  15.7 11.4 %copy-start.2 = (bf16[7,32,1536]{2,1,0:T(8,128)(2,1)}, bf16[7,32,1536]{2,1,0:T(8,128)(2,1)S(1)}, u32[]{:S(2)}) copy-start(bf16[7,32,1536]{2,1,0:T(8,128)(2,1)S(1)} %get-tuple-element.121) | copy-start | bytes 2064388
  28.5 8.7 %slice-start.2 = ((s8[4718592]{0:T(1024)(128)(4,1)}), s8[4194304]{0:T(1024)(128)(4,1)S(1)}, s32[]{:S(2)}) async-start(s8[4718592]{0:T(1024)(128)(4,1)} %bitcast.86), calls=%async_computation.7 | async-start | bytes 8388608
  29.5 7.8 %slice-start.3 = ((s8[4718592]{0:T(1024)(128)(4,1)}), s8[524288]{0:T(1024)(128)(4,1)S(1)}, s32[]{:S(2)}) async-start(s8[4718592]{0:T(1024)(128)(4,1)} %bitcast.86), calls=%async_computation.8 | async-start | bytes 1048576
  29.5 10.2 %slice-start = ((s8[4718592]{0:T(1024)(128)(4,1)}), s8[4194304]{0:T(1024)(128)(4,1)S(1)}, s32[]{:S(2)}) async-start(s8[4718592]{0:T(1024)(128)(4,1)} %bitcast.81), calls=%async_computation.5 | async-start | bytes 8388608
  42.1 82.8 %reduce-scatter.7.cloned.1.call-start = ((), (), s32[]{:S(2)}) async-start(), calls=%async_computation.3 | async-start | bytes 5898240
  53.6 106.1 %reduce-scatter.5.cloned.1.call-start = ((), (), s32[]{:S(2)}) async-start(), calls=%async_computation.2 | async-start | bytes 5898240 | tf_op jit(solution)/shard_map/reduce_scatter | solution.py:85
  58.5 32.9 %copy-start.84 = (f32[128]{0:T(128)S(1)}, f32[128]{0:T(128)}, u32[]{:S(2)}) copy-start(f32[128]{0:T(128)} %div.15) | copy-start | bytes 1540
  58.5 32.9 %copy-start.85 = (f32[128]{0:T(128)S(1)}, f32[128]{0:T(128)}, u32[]{:S(2)}) copy-start(f32[128]{0:T(128)} %rsqrt.12) | copy-start | bytes 1540
  99.5 15.2 %copy-start.7 = (bf16[128,1536]{1,0:T(8,128)(2,1)S(1)}, bf16[128,1536]{1,0:T(8,128)(2,1)}, u32[]{:S(2)}) copy-start(bf16[128,1536]{1,0:T(8,128)(2,1)} %get-tuple-element.114) | copy-start | bytes 1179652
  109.9 7.3 %copy-start.5 = (bf16[4,32,1536]{2,1,0:T(8,128)(2,1)S(1)}, bf16[4,32,1536]{2,1,0:T(8,128)(2,1)}, u32[]{:S(2)}) copy-start(bf16[4,32,1536]{2,1,0:T(8,128)(2,1)} %param.9) | copy-start | bytes 1179652
  109.9 7.3 %copy-start.9 = (f32[1536]{0:T(1024)S(1)}, f32[1536]{0:T(1024)}, u32[]{:S(2)}) copy-start(f32[1536]{0:T(1024)} %copy-done.8) | copy-start | bytes 18436
  109.9 7.3 %copy-start.11 = (f32[1536]{0:T(1024)S(1)}, f32[1536]{0:T(1024)}, u32[]{:S(2)}) copy-start(f32[1536]{0:T(1024)} %copy-done.10) | copy-start | bytes 18436
  109.9 7.3 %copy-start.13 = (f32[1536]{0:T(1024)S(1)}, f32[1536]{0:T(1024)}, u32[]{:S(2)}) copy-start(f32[1536]{0:T(1024)} %copy-done.12) | copy-start | bytes 18436
  109.9 7.3 %copy-start.15 = (f32[1536]{0:T(1024)S(1)}, f32[1536]{0:T(1024)}, u32[]{:S(2)}) copy-start(f32[1536]{0:T(1024)} %copy-done.14) | copy-start | bytes 18436
  109.9 7.3 %copy-start.17 = (f32[1536]{0:T(1024)S(1)}, f32[1536]{0:T(1024)}, u32[]{:S(2)}) copy-start(f32[1536]{0:T(1024)} %copy-done.16) | copy-start | bytes 18436
  109.9 7.3 %copy-start.19 = (f32[1536]{0:T(1024)S(1)}, f32[1536]{0:T(1024)}, u32[]{:S(2)}) copy-start(f32[1536]{0:T(1024)} %copy-done.18) | copy-start | bytes 18436
  109.9 7.3 %copy-start.21 = (f32[1536]{0:T(1024)S(1)}, f32[1536]{0:T(1024)}, u32[]{:S(2)}) copy-start(f32[1536]{0:T(1024)} %copy-done.20) | copy-start | bytes 18436
  109.9 7.3 %copy-start.23 = (f32[1536]{0:T(1024)S(1)}, f32[1536]{0:T(1024)}, u32[]{:S(2)}) copy-start(f32[1536]{0:T(1024)} %copy-done.22) | copy-start | bytes 18436
  109.9 7.3 %copy-start.25 = (f32[1536]{0:T(1024)S(1)}, f32[1536]{0:T(1024)}, u32[]{:S(2)}) copy-start(f32[1536]{0:T(1024)} %copy-done.24) | copy-start | bytes 18436
  110.0 7.3 %copy-start.27 = (f32[1536]{0:T(1024)S(1)}, f32[1536]{0:T(1024)}, u32[]{:S(2)}) copy-start(f32[1536]{0:T(1024)} %copy-done.26) | copy-start | bytes 18436
  110.0 7.3 %copy-start.29 = (f32[1536]{0:T(1024)S(1)}, f32[1536]{0:T(1024)}, u32[]{:S(2)}) copy-start(f32[1536]{0:T(1024)} %copy-done.28) | copy-start | bytes 18436
  110.0 7.3 %copy-start.31 = (f32[1536]{0:T(1024)S(1)}, f32[1536]{0:T(1024)}, u32[]{:S(2)}) copy-start(f32[1536]{0:T(1024)} %copy-done.30) | copy-start | bytes 18436
  110.0 7.3 %copy-start.33 = (f32[1536]{0:T(1024)S(1)}, f32[1536]{0:T(1024)}, u32[]{:S(2)}) copy-start(f32[1536]{0:T(1024)} %copy-done.32) | copy-start | bytes 18436
  110.0 7.3 %copy-start.35 = (f32[1536]{0:T(1024)S(1)}, f32[1536]{0:T(1024)}, u32[]{:S(2)}) copy-start(f32[1536]{0:T(1024)} %copy-done.34) | copy-start | bytes 18436
  110.0 7.3 %copy-start.37 = (f32[1536]{0:T(1024)S(1)}, f32[1536]{0:T(1024)}, u32[]{:S(2)}) copy-start(f32[1536]{0:T(1024)} %copy-done.36) | copy-start | bytes 18436
  110.0 7.3 %copy-start.39 = (f32[1536]{0:T(1024)S(1)}, f32[1536]{0:T(1024)}, u32[]{:S(2)}) copy-start(f32[1536]{0:T(1024)} %copy-done.38) | copy-start | bytes 18436
  111.0 4.5 %collective-permute-start.2 = (bf16[3,32,1536]{2,1,0:T(8,128)(2,1)S(1)}, bf16[3,32,1536]{2,1,0:T(8,128)(2,1)S(1)}, u32[]{:S(2)}, u32[]{:S(2)}) collective-permute-start(bf16[3,32,1536]{2,1,0:T(8,128)(2,1)S(1)} %bitcast.93), channel_id=1, source_target_pairs={{0,1},{1,2},{2,3},{4,5},{5,6},{6,7},{8,9},{9,10},{10,11},{12,13},{... | collective-permute-start | bytes 884744 | tf_op jit(solution)/shard_map/ppermute | solution.py:14
  113.3 3.5 %collective-permute-start.3 = (bf16[3,32,1536]{2,1,0:T(8,128)(2,1)S(1)}, bf16[3,32,1536]{2,1,0:T(8,128)(2,1)S(1)}, u32[]{:S(2)}, u32[]{:S(2)}) collective-permute-start(bf16[3,32,1536]{2,1,0:T(8,128)(2,1)S(1)} %bitcast.92), channel_id=1, source_target_pairs={{1,0},{2,1},{3,2},{5,4},{6,5},{7,6},{9,8},{10,9},{11,10},{13,12},{... | collective-permute-start | bytes 884744 | tf_op jit(solution)/shard_map/ppermute | solution.py:17
  (49 other events, 251.9 us)
Sparse Core Ops, SparseCore 0:
  42.2 49.0 all-reduce.4
Sparse Core Ops, SparseCore 1:
  53.7 53.9 reduce-scatter.6
  110.2 49.4 reduce-scatter.4
